TPU v7x, 32 devices: a whole 2x2x4 slice. The times are simulated.
32 devices in a mesh: section: 2 (over x), wafer: 4 (over y, core), sub: 4 (over z).
Axes of the slice: x: 2, y: 2, z: 4, core: 2. Of those that a mesh axis runs over, the one named last changes fastest.
Arguments:
- tod: float32 [1, 256, 2048], P(None, 'wafer', ('section', 'sub')), may hold values from -6 to 6
- templates: float32 [1, 256, 2048], P(None, 'wafer', ('section', 'sub'))
- det_weight: float32 [256], P('wafer'), may hold values from 0.3 to 3
- pixel: int32 [1, 256, 2048], P(None, 'wafer', ('section', 'sub')), may hold values from 0 to 511
- hitlist: int32 [1, 64, 128], P(None, 'wafer', ('section', 'sub')), may hold values from 0 to 127, as said below
- counts: int32 [1, 64, 8], P(None, 'wafer', ('section', 'sub')), may hold values from 2 to 16
Outputs:
- sky_map: float32 [8192], P(('wafer', 'sub'))
Inputs may be any that keep to these rules, and one draw needn't show every extreme that they name: `hitlist`: for each micro-batch, source device and tile, the live slots name distinct blocks of that source, and no block is named by live slots of two tiles; in each micro-batch exactly one tile has a full hit list (all 16 slots live) from every source device.
All inputs are finite; a program needn't handle non-finite values.
Results may differ from a plain program's by a relative error of at most 0.0003.
Values sent between devices are 32-bit elements; how exact they have to be, the bound alone decides.
A program may use at most 64 MiB of HBM per device.

v0:
```python
import jax
import jax.numpy as jnp
from jax import lax
from jax.sharding import PartitionSpec as P

BL = 128
TILE = 512


def bin_block(values, pixels, weights, tile_size):
    upper_count = tile_size // 128
    row_count = values.shape[0]
    upper_part = pixels // 128
    lower_part = pixels % 128
    upper_hot = (
        lax.broadcasted_iota(jnp.int32, (upper_count, row_count), 0) == upper_part[None, :]
    ).astype(jnp.float32)
    lower_hot = (
        lax.broadcasted_iota(jnp.int32, (row_count, 128), 1) == lower_part[:, None]
    ).astype(jnp.float32)
    stacked = jnp.concatenate([upper_hot * values[None, :], upper_hot * weights[None, :]], axis=0)
    binned = jnp.dot(
        stacked, lower_hot, precision=lax.Precision.HIGHEST, preferred_element_type=jnp.float32
    )
    return (binned[:upper_count].reshape(-1), binned[upper_count:].reshape(-1))


def shards(tod, templates, det_weight, pixel, hitlist, counts):
    samp_local = tod.shape[2]
    owners = hitlist.shape[1]
    slots = hitlist.shape[2]
    per_det = samp_local // BL
    tile_size = TILE
    slot_ids = lax.broadcasted_iota(jnp.int32, (owners, slots), 1)
    block_weight = jnp.repeat(det_weight, per_det)
    num_tile = jnp.zeros((tile_size,), jnp.float32)
    wgt_tile = jnp.zeros((tile_size,), jnp.float32)

    def add_source(carry, inputs_now):
        num_part, wgt_part = bin_block(inputs_now[0], inputs_now[1], inputs_now[2], tile_size)
        return ((carry[0] + num_part, carry[1] + wgt_part), None)

    template_rows = templates[0]
    streams = tod[0]
    gram_sum = lax.dot_general(
        template_rows,
        template_rows,
        (((1,), (1,)), ((), ())),
        precision=lax.Precision.HIGHEST,
        preferred_element_type=jnp.float32,
    )
    projection = lax.dot_general(
        template_rows,
        streams,
        (((1,), (1,)), ((), ())),
        precision=lax.Precision.HIGHEST,
        preferred_element_type=jnp.float32,
    )
    gram_sum, projection = lax.psum((gram_sum, projection), ("section", "sub"))
    factor = jnp.linalg.cholesky(gram_sum)
    coef_fit = jax.scipy.linalg.cho_solve((factor, True), projection)
    removed = lax.dot_general(
        coef_fit,
        template_rows,
        (((0,), (0,)), ((), ())),
        precision=lax.Precision.HIGHEST,
        preferred_element_type=jnp.float32,
    )
    filtered = streams - removed
    weighted = (filtered * det_weight[:, None]).reshape(-1, BL)
    pixel_blocks = pixel[0].reshape(-1, BL)
    hit_rows = hitlist[0]
    live_slots = slot_ids < counts[0]
    send_values = jnp.where(live_slots[:, :, None], weighted[hit_rows], 0.0)
    send_pixels = jnp.where(live_slots[:, :, None], pixel_blocks[hit_rows], 0)
    send_weights = jnp.where(live_slots, block_weight[hit_rows], 0.0)
    got_values = lax.all_to_all(
        send_values, ("wafer", "sub"), split_axis=0, concat_axis=0, tiled=True
    )
    got_pixels = lax.all_to_all(
        send_pixels, ("wafer", "sub"), split_axis=0, concat_axis=0, tiled=True
    )
    got_weights = lax.all_to_all(
        send_weights, ("wafer", "sub"), split_axis=0, concat_axis=0, tiled=True
    )
    full_weights = jnp.broadcast_to(got_weights[..., None], got_values.shape)
    row_len = slots * BL
    (num_tile, wgt_tile), unused = lax.scan(
        add_source,
        (num_tile, wgt_tile),
        (
            got_values.reshape(-1, row_len),
            got_pixels.reshape(-1, row_len),
            full_weights.reshape(-1, row_len),
        ),
    )
    num_tile, wgt_tile = lax.psum((num_tile, wgt_tile), "section")
    return num_tile / jnp.maximum(wgt_tile, 1.0)


def solution(mesh):
    placed = (
        P(None, "wafer", ("section", "sub")),
        P(None, "wafer", ("section", "sub")),
        P("wafer"),
        P(None, "wafer", ("section", "sub")),
        P(None, "wafer", ("section", "sub")),
        P(None, "wafer", ("section", "sub")),
    )
    return jax.shard_map(
        shards, mesh=mesh, in_specs=placed, out_specs=P(("wafer", "sub")), check_vma=False
    )
```

profile of v0, /device:TPU:0, one launch (start us, length us, event | category | flops | bytes accessed | tf_op | source)
XLA Modules:
  0.0 105.2 jit_solution(3944676223906672831)
XLA Ops:
  0.0 0.7 compare_select_fusion.4
  0.8 0.6 copy-done.3
  1.7 1.9 %gather_fusion.2 = f32[256]{0:T(256)S(1)} fusion(f32[128]{0:T(128)S(1)} %reshape.153, s32[1024]{0:T(1024)S(1)} %pad_clamp_fusion), kind=kCustom, calls=%fused_computation.2 | custom fusion | bytes 3072 | tf_op jit(solution)/shard_map/gather | solution.py:76
  3.7 0.6 copy-done.4
  4.3 0.7 compare_select_fusion.3
  5.0 7.4 %all-to-all-start.2 = ((f32[16,1,16]{2,1,0:T(1,128)}), f32[16,1,16]{2,1,0:T(1,128)S(1)}, u32[]{:S(2)}, u32[]{:S(2)}) async-start(f32[16,1,16]{2,1,0:T(1,128)} %compare_select_fusion.3), calls=%async_computation.2 | async-start | bytes 16384 | tf_op jit(solution)/shard_map/all_to_all | solution.py:83
  12.9 38.5 %all-reduce = (f32[64,64]{1,0:T(8,128)S(1)}, f32[64,64]{0,1:T(8,128)S(1)}) all-reduce(f32[64,64]{1,0:T(8,128)S(1)} %fusion.11, f32[64,64]{0,1:T(8,128)S(1)} %fusion.13), channel_id=1, replica_groups=mesh['section'=2,'wafer'=4,'sub'=4] {'section','sub'}, use_global_device_ids=true, to_apply=%region_3.4 | all-reduce | flops 8192 | bytes 65536 | tf_op jit(solution)/shard_map/psum | solution.py:59
  51.5 5.8 %cholesky.16 = f32[64,64]{1,0:T(8,128)S(1)} custom-call(f32[64,64]{1,0:T(8,128)S(1)} %fusion.21), custom_call_target="Cholesky" | custom-call | tf_op jit(solution)/shard_map/jit(cholesky)/cholesky | solution.py:60
  57.4 0.6 compare_reduce_fusion
  58.0 0.7 fusion.16
  58.7 4.9 %custom-call.10 = f32[1,64,64]{1,2,0:T(8,128)S(1)} custom-call(f32[1,64,64]{2,1,0:T(8,128)S(1)} %fusion.16), custom_call_target="InvertDiagBlocksLowerTriangular" | custom-call | tf_op jit(solution)/shard_map/jit(_cho_solve)/triangular_solve | solution.py:61
  64.3 0.7 gather_fusion.1
  65.0 0.7 broadcast_select_fusion
  65.8 3.6 %all-to-all-start.1 = ((f32[16,16,128]{2,1,0:T(8,128)}), f32[16,16,128]{2,1,0:T(8,128)S(1)}, u32[]{:S(2)}, u32[]{:S(2)}) async-start(f32[16,16,128]{2,1,0:T(8,128)} %broadcast_select_fusion), calls=%async_computation.1 | async-start | bytes 262144 | tf_op jit(solution)/shard_map/all_to_all | solution.py:77
  69.5 0.7 gather_fusion
  70.2 0.8 broadcast_select_fusion.1
  70.9 5.8 %all-to-all-done.1 = f32[16,16,128]{2,1,0:T(8,128)S(1)} async-done(((f32[16,16,128]{2,1,0:T(8,128)}), f32[16,16,128]{2,1,0:T(8,128)S(1)}, u32[]{:S(2)}, u32[]{:S(2)}) %all-to-all-start.1) | async-done | bytes 131104 | tf_op jit(solution)/shard_map/all_to_all | solution.py:77
  76.7 3.5 %all-to-all-start = ((s32[16,16,128]{2,1,0:T(8,128)}), s32[16,16,128]{2,1,0:T(8,128)S(1)}, u32[]{:S(2)}, u32[]{:S(2)}) async-start(s32[16,16,128]{2,1,0:T(8,128)} %broadcast_select_fusion.1), calls=%async_computation | async-start | bytes 262144 | tf_op jit(solution)/shard_map/all_to_all | solution.py:80
  80.5 7.1 %all-to-all-done = s32[16,16,128]{2,1,0:T(8,128)S(1)} async-done(((s32[16,16,128]{2,1,0:T(8,128)}), s32[16,16,128]{2,1,0:T(8,128)S(1)}, u32[]{:S(2)}, u32[]{:S(2)}) %all-to-all-start) | async-done | bytes 131104 | tf_op jit(solution)/shard_map/all_to_all | solution.py:80
  87.6 12.0 %while.15 = (s32[]{:T(128)}, f32[512]{0:T(512)S(1)}, f32[512]{0:T(512)S(1)}, s32[16,2048]{1,0:T(8,128)S(1)}, f32[16,2048]{1,0:T(8,128)S(1)}, /*index=5*/f32[16,2048]{1,0:T(8,128)S(1)}, s32[]{:T(128)}, s32[]{:T(128)}) while((s32[]{:T(128)}, f32[512]{0:T(512)S(1)}, f32[512]{0:T(512)S(1)}, s32[16,2048]{1,0:T(8,128)S(1)}, ...), condition=%wide.region_5.6_spmd.clone, body=%wide.region_4.5_spmd.clone.sunk | while | flops 25524224 | bytes 254055 | solution.py:88
  87.8 0.6 fusion.30
  88.5 0.6 fusion.30
  99.6 4.9 %all-reduce.1 = (f32[512]{0:T(512)S(1)}, f32[512]{0:T(512)S(1)}) all-reduce(f32[512]{0:T(512)S(1)} %get-tuple-element.86, f32[512]{0:T(512)S(1)} %get-tuple-element.87), channel_id=1, replica_groups=mesh['section'=2,'wafer'=4,'sub'=4] {'section'}, use_global_device_ids=true, to_apply=%region_6.7 | all-reduce | flops 1024 | bytes 8192 | tf_op jit(solution)/shard_map/psum | solution.py:97
  104.6 0.6 maximum_divide_fusion
  (125 shorter events, 11.9 us)
Async XLA Ops:
  0.0 12.5 %copy-start = (f32[1,64,256]{2,1,0:T(8,128)S(1)}, f32[1,64,256]{2,1,0:T(8,128)}, u32[]{:S(2)}) copy-start(f32[1,64,256]{2,1,0:T(8,128)} %param.9) | copy-start | bytes 196612
  0.8 0.7 copy-start.3
  3.7 0.7 copy-start.4
  4.3 8.4 %copy-start.1 = (f32[1,64,256]{2,1,0:T(8,128)S(1)}, f32[1,64,256]{2,1,0:T(8,128)}, u32[]{:S(2)}) copy-start(f32[1,64,256]{2,1,0:T(8,128)} %param.8) | copy-start | bytes 196612
  5.0 60.8 %all-to-all-start.2 = ((f32[16,1,16]{2,1,0:T(1,128)}), f32[16,1,16]{2,1,0:T(1,128)S(1)}, u32[]{:S(2)}, u32[]{:S(2)}) async-start(f32[16,1,16]{2,1,0:T(1,128)} %compare_select_fusion.3), calls=%async_computation.2 | async-start | bytes 16384 | tf_op jit(solution)/shard_map/all_to_all | solution.py:83
  65.8 3.7 %copy-start.2 = (s32[1,64,256]{2,1,0:T(8,128)S(1)}, s32[1,64,256]{2,1,0:T(8,128)}, u32[]{:S(2)}) copy-start(s32[1,64,256]{2,1,0:T(8,128)} %param.11) | copy-start | bytes 196612
  65.8 11.0 %all-to-all-start.1 = ((f32[16,16,128]{2,1,0:T(8,128)}), f32[16,16,128]{2,1,0:T(8,128)S(1)}, u32[]{:S(2)}, u32[]{:S(2)}) async-start(f32[16,16,128]{2,1,0:T(8,128)} %broadcast_select_fusion), calls=%async_computation.1 | async-start | bytes 262144 | tf_op jit(solution)/shard_map/all_to_all | solution.py:77
  76.7 10.8 %all-to-all-start = ((s32[16,16,128]{2,1,0:T(8,128)}), s32[16,16,128]{2,1,0:T(8,128)S(1)}, u32[]{:S(2)}, u32[]{:S(2)}) async-start(s32[16,16,128]{2,1,0:T(8,128)} %broadcast_select_fusion.1), calls=%async_computation | async-start | bytes 262144 | tf_op jit(solution)/shard_map/all_to_all | solution.py:80
where the time goes:
time: 106 us; the launch traced here: 105 us
  blocking collectives  43.5 us (41%)
  other arithmetic  17.3 us (16%)
  starting transfers between devices  14.5 us (14%)
  waiting for transfers between devices  12.9 us (12%)
  matrix products  10.3 us (10%)
  local copies, waits for them, and re-layouts  5.65 us (5%)
    psum x1, blocking collectives, shards(): gram_sum, projection = lax.psum((gram_sum, projection), ('section', 'sub'))  38.5 us
    dot_general x16, matrix products, bin_block(): jnp.dot(stacked, lower_hot, precision=lax.Precision.HIGHEST, preferred_el...  9.19 us
    all_to_all x1, starting transfers between devices, shards(): lax.all_to_all(send_weights, ('wafer', 'sub'), split_axis=0, concat_axis=...  7.39 us
    all_to_all x1, waiting for transfers between devices, shards(): lax.all_to_all(send_pixels, ('wafer', 'sub'), split_axis=0, concat_axis=0...  7.09 us
    another operation x3, other arithmetic, shards(): factor = jnp.linalg.cholesky(gram_sum)  6.52 us
    all_to_all x1, waiting for transfers between devices, shards(): lax.all_to_all(send_values, ('wafer', 'sub'), split_axis=0, concat_axis=0...  5.8 us
    another operation x2, other arithmetic, shards(): coef_fit = jax.scipy.linalg.cho_solve((factor, True), projection)  5.55 us
    psum x1, blocking collectives, shards(): num_tile, wgt_tile = lax.psum((num_tile, wgt_tile), 'section')  4.94 us
  transfers between devices with their start and end apart: 3, of which 2 were waited for; matrix products, arithmetic and copies ran while one was open for 16% of the time, Pallas kernels for 0%

commit v1 on v0

v1 whole, which is shorter than its diff:
```python
import functools

import jax
import jax.numpy as jnp
from jax import lax
from jax.experimental import pallas as pl
from jax.experimental.pallas import tpu as pltpu
from jax.sharding import PartitionSpec as P

BL = 128
TILE = 512
LANES = 128
MESH = pl.DeviceIdType.MESH
HIGHEST = lax.Precision.HIGHEST


def solve_augmented(blocks, unknowns):
    row = lax.broadcasted_iota(jnp.int32, blocks[0].shape, 0)
    shape = blocks[0].shape
    for kb in range(unknowns // 8):
        cols = [
            [jnp.broadcast_to(b[:, kb * 8 + t : kb * 8 + t + 1], shape) for t in range(8)]
            for b in blocks
        ]
        rows = blocks[kb]
        c = list(cols[kb])
        for t in range(8):
            inv = 1.0 / c[t][t : t + 1, :]
            scaled = rows[t : t + 1, :] * inv
            rows = jnp.where(row == t, scaled, rows - c[t] * scaled)
            for s in range(t + 1, 8):
                m = c[s][t : t + 1, :] * inv
                c[s] = jnp.where(row == t, m, c[s] - c[t] * m)
        for rb in range(len(blocks)):
            if rb == kb:
                continue
            b = blocks[rb]
            for t in range(8):
                b = b - cols[rb][t] * rows[t : t + 1, :]
            blocks[rb] = b
        blocks[kb] = rows
    return blocks


def kernel(
    sizes,
    tod_ref,
    tmpl_ref,
    weight_ref,
    pixel_ref,
    hit_ref,
    count_ref,
    out_ref,
    aug,
    red_in,
    full,
    upper,
    lower,
    vals_hi,
    vals_lo,
    num_out,
    wgt_out,
    num_in,
    wgt_in,
    red_send,
    red_recv,
    all_send,
    all_recv,
    wgt_send,
    wgt_recv,
    num_send,
    num_recv,
):
    n_sec, n_waf, n_sub = sizes
    group = n_sec * n_sub
    total = group * n_waf
    sec, waf, sub = (lax.axis_index(a) for a in ("section", "wafer", "sub"))
    me_group = sec * n_sub + sub
    me = (sec * n_waf + waf) * n_sub + sub
    my_tile = waf * n_sub + sub
    dets, samp = tod_ref.shape
    templ = tmpl_ref.shape[0]
    owners, slots = hit_ref.shape
    per_det = samp // BL
    up_count = TILE // LANES
    rows_up = owners * up_count
    part = templ // group

    def group_peer(step):
        g = lax.rem(me_group + step, group)
        return g, (g // n_sub, waf, lax.rem(g, n_sub))

    def any_peer(step):
        g = lax.rem(me + step, total)
        dev = (g // (n_waf * n_sub), lax.rem(g // n_sub, n_waf), lax.rem(g, n_sub))
        return lax.rem(g, n_waf * n_sub), dev

    barrier = pltpu.get_barrier_semaphore()

    @pl.loop(1, total)
    def _(step):
        pl.semaphore_signal(barrier, inc=1, device_id=any_peer(step)[1], device_id_type=MESH)

    modes = tmpl_ref[...]
    both = jnp.concatenate([modes, tod_ref[...]], axis=0)
    local = lax.dot_general(
        modes, both, (((1,), (1,)), ((), ())), precision=HIGHEST,
        preferred_element_type=jnp.float32,
    )
    aug[...] = local.reshape(aug.shape)
    pl.semaphore_wait(barrier, total - 1)

    @pl.loop(1, group)
    def _(step):
        g, dev = group_peer(step)
        pltpu.make_async_remote_copy(
            src_ref=aug.at[g], dst_ref=red_in.at[step - 1],
            send_sem=red_send, recv_sem=red_recv, device_id=dev, device_id_type=MESH,
        ).start()

    nblk = dets * per_det
    hits = hit_ref[...]
    live = count_ref[...]
    blk = lax.broadcasted_iota(jnp.int32, (owners, nblk), 1)
    owner_id = lax.broadcasted_iota(jnp.int32, (owners, nblk), 0) + 1
    named = jnp.zeros((owners, nblk), jnp.int32)
    for j in range(slots):
        named = jnp.where((hits[:, j : j + 1] == blk) & (live > j), owner_id, named)
    tile_row = jnp.sum(named.astype(jnp.float32), axis=0, keepdims=True)
    tile_row = jnp.broadcast_to(tile_row, (BL, nblk))
    pick_d = lax.broadcasted_iota(jnp.int32, (dets, nblk), 0)
    pick_b = lax.broadcasted_iota(jnp.int32, (dets, nblk), 1)
    pixels = pixel_ref[...]
    tiles = []
    for h in range(per_det):
        pick = (pick_b == pick_d * per_det + h).astype(jnp.float32)
        tiles.append(
            lax.dot_general(
                pick, tile_row, (((1,), (1,)), ((), ())), precision=HIGHEST,
                preferred_element_type=jnp.float32,
            )
        )
    tile = jnp.concatenate(tiles, axis=1).astype(jnp.int32) - 1
    up = tile * up_count + lax.shift_right_logical(pixels, 7)
    upper[...] = jnp.where(tile < 0, -1, up)
    lower[...] = jnp.bitwise_and(pixels, LANES - 1)

    eye_r = lax.broadcasted_iota(jnp.int32, (dets, dets), 0)
    eye_c = lax.broadcasted_iota(jnp.int32, (dets, dets), 1)
    weight = jnp.sum(
        jnp.where(eye_r == eye_c, jnp.broadcast_to(weight_ref[...], (dets, dets)), 0.0),
        axis=1, keepdims=True,
    )
    weight = jnp.broadcast_to(weight, (dets, samp))

    def split(values):
        hi = values.astype(jnp.bfloat16).astype(jnp.float32)
        vals_hi[...] = hi
        vals_lo[...] = values - hi

    def bin_all():
        up_iota = lax.broadcasted_iota(jnp.int32, (rows_up, samp), 0)
        low_iota = lax.broadcasted_iota(jnp.int32, (LANES, samp), 0)

        def body(c, acc):
            d0 = pl.multiple_of(c * 8, 8)
            u8 = upper[pl.ds(d0, 8), :]
            l8 = lower[pl.ds(d0, 8), :]
            h8 = vals_hi[pl.ds(d0, 8), :]
            o8 = vals_lo[pl.ds(d0, 8), :]
            lhs, rhs = [], []
            for i in range(8):
                hot = u8[i : i + 1, :] == up_iota
                a_hi = jnp.where(hot, h8[i : i + 1, :], 0.0).astype(jnp.bfloat16)
                a_lo = jnp.where(hot, o8[i : i + 1, :], 0.0).astype(jnp.bfloat16)
                lhs.append(jnp.concatenate([a_hi, a_lo], axis=0))
                rhs.append((l8[i : i + 1, :] == low_iota).astype(jnp.float32).astype(jnp.bfloat16))
            return acc + lax.dot_general(
                jnp.concatenate(lhs, axis=1), jnp.concatenate(rhs, axis=1),
                (((1,), (1,)), ((), ())), preferred_element_type=jnp.float32,
            )

        acc = lax.fori_loop(0, dets // 8, body, jnp.zeros((2 * rows_up, LANES), jnp.float32))
        return (acc[:rows_up] + acc[rows_up:]).reshape(owners, up_count, LANES)

    def send_tiles(out, landing, send_sem, recv_sem):
        @pl.loop(1, total)
        def _(step):
            o, dev = any_peer(step)
            pltpu.make_async_remote_copy(
                src_ref=out.at[o], dst_ref=landing.at[step - 1],
                send_sem=send_sem, recv_sem=recv_sem, device_id=dev, device_id_type=MESH,
            ).start()

    def wait_all(ref, sem):
        pltpu.make_async_copy(ref, ref, sem).wait()

    wait_all(red_in, red_recv)
    mine = aug[me_group]
    for step in range(group - 1):
        mine = mine + red_in[step]
    full[me_group] = mine

    @pl.loop(1, group)
    def _(step):
        g, dev = group_peer(step)
        pltpu.make_async_remote_copy(
            src_ref=full.at[me_group], dst_ref=full.at[me_group],
            send_sem=all_send, recv_sem=all_recv, device_id=dev, device_id_type=MESH,
        ).start()

    split(weight)
    wgt_out[...] = bin_all()
    send_tiles(wgt_out, wgt_in, wgt_send, wgt_recv)
    wait_all(red_in, all_recv)

    system = full[...].reshape(templ, templ + dets)
    blocks = [system[8 * b : 8 * b + 8, :] for b in range(templ // 8)]
    coef = jnp.concatenate(solve_augmented(blocks, templ), axis=0)[:, templ:]
    removed = lax.dot_general(
        coef, tmpl_ref[...], (((0,), (0,)), ((), ())), precision=HIGHEST,
        preferred_element_type=jnp.float32,
    )
    split((tod_ref[...] - removed) * weight)
    num_out[...] = bin_all()
    send_tiles(num_out, num_in, num_send, num_recv)

    wait_all(wgt_in, wgt_recv)
    wgt = wgt_out[my_tile] + jnp.sum(wgt_in[...], axis=0)
    wait_all(num_in, num_recv)
    num = num_out[my_tile] + jnp.sum(num_in[...], axis=0)
    out_ref[...] = num / jnp.maximum(wgt, 1.0)

    wait_all(red_in, red_send)
    wait_all(red_in, all_send)
    wait_all(wgt_in, wgt_send)
    wait_all(num_in, num_send)


def shards(sizes, tod, templates, det_weight, pixel, hitlist, counts):
    n_sec, n_waf, n_sub = sizes
    group = n_sec * n_sub
    total = group * n_waf
    dets, samp = tod.shape[1:]
    templ = templates.shape[1]
    owners = hitlist.shape[1]
    part = templ // group
    up_count = TILE // LANES
    vmem = pl.BlockSpec(memory_space=pltpu.VMEM)
    f32, i32 = jnp.float32, jnp.int32
    wide = templ + dets
    out = pl.pallas_call(
        functools.partial(kernel, sizes),
        out_shape=jax.ShapeDtypeStruct((up_count, LANES), f32),
        in_specs=[vmem] * 6,
        out_specs=vmem,
        scratch_shapes=[
            pltpu.VMEM((group, part, wide), f32),
            pltpu.VMEM((group - 1, part, wide), f32),
            pltpu.VMEM((group, part, wide), f32),
            pltpu.VMEM((dets, samp), i32),
            pltpu.VMEM((dets, samp), i32),
            pltpu.VMEM((dets, samp), f32),
            pltpu.VMEM((dets, samp), f32),
            pltpu.VMEM((owners, up_count, LANES), f32),
            pltpu.VMEM((owners, up_count, LANES), f32),
            pltpu.VMEM((total - 1, up_count, LANES), f32),
            pltpu.VMEM((total - 1, up_count, LANES), f32),
        ]
        + [pltpu.SemaphoreType.DMA] * 8,
        compiler_params=pltpu.CompilerParams(
            collective_id=0, has_side_effects=True, vmem_limit_bytes=32 * 1024 * 1024
        ),
    )(tod[0], templates[0], det_weight[None, :], pixel[0], hitlist[0], counts[0])
    return out.reshape(-1)


def solution(mesh):
    sizes = tuple(mesh.shape[a] for a in ("section", "wafer", "sub"))
    placed = (
        P(None, "wafer", ("section", "sub")),
        P(None, "wafer", ("section", "sub")),
        P("wafer"),
        P(None, "wafer", ("section", "sub")),
        P(None, "wafer", ("section", "sub")),
        P(None, "wafer", ("section", "sub")),
    )
    return jax.shard_map(
        functools.partial(shards, sizes), mesh=mesh, in_specs=placed,
        out_specs=P(("wafer", "sub")), check_vma=False,
    )
```

time: 106 us -> 28.3 us (0.27)
  blocking collectives: 43.5 us -> 0 us
  Pallas kernels: 0 us -> 23.6 us
  other arithmetic: 17.3 us -> 0 us
  starting transfers between devices: 14.5 us -> 0 us
  waiting for transfers between devices: 12.9 us -> 0 us
  matrix products: 10.3 us -> 0 us
  local copies, waits for them, and re-layouts: 5.65 us -> 4.41 us
    psum x2 -> x0, blocking collectives: 43.5 us -> none  [the longest x1 38.5 us: shards(): gram_sum, projection = lax.psum((gram_sum, projection), ('section', 'sub'))]
    pallas_call x0 -> x1, Pallas kernels: none -> 23.6 us  [shards(): pl.pallas_call(functools.partial(kernel, sizes), out_shape=jax.ShapeDtype...]
    all_to_all x3 -> x0, starting transfers between devices: 14.5 us -> none  [the longest x1 7.39 us: shards(): lax.all_to_all(send_weights, ('wafer', 'sub'), split_axis=0, concat_axis=...]
    all_to_all x3 -> x0, waiting for transfers between devices: 12.9 us -> none  [the longest x1 7.09 us: shards(): lax.all_to_all(send_pixels, ('wafer', 'sub'), split_axis=0, concat_axis=0...]
    another operation x5 -> x0, other arithmetic: 12.1 us -> none  [the longest x3 6.52 us: shards(): factor = jnp.linalg.cholesky(gram_sum)]
    dot_general x19 -> x0, matrix products: 9.85 us -> none  [the longest x16 9.19 us: bin_block(): jnp.dot(stacked, lower_hot, precision=lax.Precision.HIGHEST, preferred_el...]
    select_n x36 -> x0, other arithmetic: 3.92 us -> none  [the longest x2 1.48 us: shards(): send_values = jnp.where(live_slots[:, :, None], weighted[hit_rows], 0.0)]
    gather x4 -> x0, local copies, waits for them, and re-layouts: 3.42 us -> none  [the longest x2 1.96 us: shards(): send_weights = jnp.where(live_slots, block_weight[hit_rows], 0.0)]
  transfers between devices with their start and end apart: 3 -> 0, of which waited for: 2 -> 0; matrix products, arithmetic and copies ran while one was open for 16% -> 0% of each run, Pallas kernels for 0% -> 0%
where the time goes in v1:
time: 28.3 us; the launch traced here: 28 us
  Pallas kernels  23.6 us (83%)
  local copies, waits for them, and re-layouts  4.41 us (16%)
    pallas_call x1, Pallas kernels, shards(): pl.pallas_call(functools.partial(kernel, sizes), out_shape=jax.ShapeDtype...  23.6 us
    unnamed x13, local copies, waits for them, and re-layouts  4.32 us

profile of v1, /device:TPU:0, one launch (start us, length us, event | category | flops | bytes accessed | tf_op | source)
XLA Modules:
  0.0 28.0 jit_solution(13626355825989749164)
XLA Ops:
  0.0 0.0 copy-start.5
  0.0 0.0 copy-start.3
  0.0 0.7 %copy-done.5 = s32[1,16,1]{1,2,0:T(1,128)S(1)} copy-done((s32[1,16,1]{1,2,0:T(1,128)S(1)}, s32[1,16,1]{1,2,0:T(1,128)}, u32[]{:S(2)}) %copy-start.5) | copy-done | bytes 88
  0.7 0.0 copy-start.4
  0.7 0.1 copy.7.count_ref
  0.7 0.0 copy-done.3
  0.7 0.6 %copy-done.4 = f32[64]{0:T(128)S(1)} copy-done((f32[64]{0:T(128)S(1)}, f32[64]{0:T(128)}, u32[]{:S(2)}) %copy-start.4) | copy-done | bytes 280
  1.3 0.0 copy-start
  1.3 0.8 %copy-done = f32[1,64,256]{2,1,0:T(8,128)S(1)} copy-done((f32[1,64,256]{2,1,0:T(8,128)S(1)}, f32[1,64,256]{2,1,0:T(8,128)}, u32[]{:S(2)}) %copy-start) | copy-done | bytes 65560
  2.2 0.0 copy-start.1
  2.2 0.8 %copy-done.1 = f32[1,64,256]{2,1,0:T(8,128)S(1)} copy-done((f32[1,64,256]{2,1,0:T(8,128)S(1)}, f32[1,64,256]{2,1,0:T(8,128)}, u32[]{:S(2)}) %copy-start.1) | copy-done | bytes 65560
  3.0 0.0 copy-start.2
  3.0 0.8 %copy-done.2 = s32[1,64,256]{2,1,0:T(8,128)S(1)} copy-done((s32[1,64,256]{2,1,0:T(8,128)S(1)}, s32[1,64,256]{2,1,0:T(8,128)}, u32[]{:S(2)}) %copy-start.2) | copy-done | bytes 65560
  3.8 23.6 %shard_map.64 = f32[4,128]{1,0:T(4,128)S(1)} custom-call(f32[64,256]{1,0:T(8,128)S(1)} %bitcast.7, f32[64,256]{1,0:T(8,128)S(1)} %bitcast.8, f32[1,64]{1,0:T(1,128)S(1)} %bitcast.12, s32[64,256]{1,0:T(8,128)S(1)} %bitcast.9, s32[16,16]{1,0:T(8,128)S(1)} %bitcast.11, s32[16,1]{1,0:T(8,128)S(1)} %copy.7.count_ref), custom_call_target="tpu_custom_call" | custom-call | tf_op jit(solution)/shard_map/pallas_call | solution.py:252
  27.4 0.6 %copy.9 = f32[512]{0:T(512)} copy(f32[512]{0:T(512)S(1)} %bitcast.10) | data formatting | bytes 4096
Async XLA Ops:
  0.0 0.7 %copy-start.5 = (s32[1,16,1]{1,2,0:T(1,128)S(1)}, s32[1,16,1]{1,2,0:T(1,128)}, u32[]{:S(2)}) copy-start(s32[1,16,1]{1,2,0:T(1,128)} %param.11) | copy-start | bytes 196
  0.0 0.7 %copy-start.3 = (s32[1,16,16]{2,1,0:T(8,128)S(1)}, s32[1,16,16]{2,1,0:T(8,128)}, u32[]{:S(2)}) copy-start(s32[1,16,16]{2,1,0:T(8,128)} %param.10) | copy-start | bytes 3076
  0.7 0.7 %copy-start.4 = (f32[64]{0:T(128)S(1)}, f32[64]{0:T(128)}, u32[]{:S(2)}) copy-start(f32[64]{0:T(128)} %param.8) | copy-start | bytes 772
  1.3 0.8 %copy-start = (f32[1,64,256]{2,1,0:T(8,128)S(1)}, f32[1,64,256]{2,1,0:T(8,128)}, u32[]{:S(2)}) copy-start(f32[1,64,256]{2,1,0:T(8,128)} %param.6) | copy-start | bytes 196612
  2.2 0.8 %copy-start.1 = (f32[1,64,256]{2,1,0:T(8,128)S(1)}, f32[1,64,256]{2,1,0:T(8,128)}, u32[]{:S(2)}) copy-start(f32[1,64,256]{2,1,0:T(8,128)} %param.7) | copy-start | bytes 196612
  3.0 0.8 %copy-start.2 = (s32[1,64,256]{2,1,0:T(8,128)S(1)}, s32[1,64,256]{2,1,0:T(8,128)}, u32[]{:S(2)}) copy-start(s32[1,64,256]{2,1,0:T(8,128)} %param.9) | copy-start | bytes 196612

commit v2 on v1

--- a/solution.py
+++ b/solution.py
@@ -44,13 +44,19 @@
 
 def kernel(
     sizes,
+    tod_hbm,
+    tmpl_hbm,
+    weight_hbm,
+    pixel_hbm,
+    hit_hbm,
+    count_hbm,
+    out_ref,
     tod_ref,
     tmpl_ref,
     weight_ref,
     pixel_ref,
     hit_ref,
     count_ref,
-    out_ref,
     aug,
     red_in,
     full,
@@ -70,6 +76,7 @@
     wgt_recv,
     num_send,
     num_recv,
+    load_sems,
 ):
     n_sec, n_waf, n_sub = sizes
     group = n_sec * n_sub
@@ -86,21 +93,59 @@
     rows_up = owners * up_count
     part = templ // group
 
+    def shifted(index, step, size):
+        if size & (size - 1) == 0:
+            return jnp.bitwise_xor(index, step)
+        return lax.rem(index + step, size)
+
+    def cut(index, size):
+        if size & (size - 1) == 0:
+            shift = size.bit_length() - 1
+            return lax.shift_right_logical(index, shift), jnp.bitwise_and(index, size - 1)
+        return index // size, lax.rem(index, size)
+
     def group_peer(step):
-        g = lax.rem(me_group + step, group)
-        return g, (g // n_sub, waf, lax.rem(g, n_sub))
+        g = shifted(me_group, step, group)
+        s, z = cut(g, n_sub)
+        return g, (s, waf, z)
 
     def any_peer(step):
-        g = lax.rem(me + step, total)
-        dev = (g // (n_waf * n_sub), lax.rem(g // n_sub, n_waf), lax.rem(g, n_sub))
-        return lax.rem(g, n_waf * n_sub), dev
-
+        g = shifted(me, step, total)
+        s, o = cut(g, n_waf * n_sub)
+        w, z = cut(o, n_sub)
+        return o, (s, w, z)
+
+    def for_peers(size, body):
+        if size <= 32:
+            for step in range(1, size):
+                body(jnp.int32(step))
+        else:
+            pl.loop(1, size)(body)
+
+    loads = [
+        pltpu.make_async_copy(src, dst, load_sems.at[i])
+        for i, (src, dst) in enumerate(
+            (
+                (tmpl_hbm, tmpl_ref),
+                (tod_hbm, tod_ref),
+                (hit_hbm, hit_ref),
+                (count_hbm, count_ref),
+                (pixel_hbm, pixel_ref),
+                (weight_hbm, weight_ref),
+            )
+        )
+    ]
+    for load in loads:
+        load.start()
     barrier = pltpu.get_barrier_semaphore()
 
-    @pl.loop(1, total)
-    def _(step):
+    def greet(step):
         pl.semaphore_signal(barrier, inc=1, device_id=any_peer(step)[1], device_id_type=MESH)
 
+    for_peers(total, greet)
+
+    loads[0].wait()
+    loads[1].wait()
     modes = tmpl_ref[...]
     both = jnp.concatenate([modes, tod_ref[...]], axis=0)
     local = lax.dot_general(
@@ -110,17 +155,28 @@
     aug[...] = local.reshape(aug.shape)
     pl.semaphore_wait(barrier, total - 1)
 
-    @pl.loop(1, group)
-    def _(step):
+    def send_rows(step):
         g, dev = group_peer(step)
         pltpu.make_async_remote_copy(
             src_ref=aug.at[g], dst_ref=red_in.at[step - 1],
             send_sem=red_send, recv_sem=red_recv, device_id=dev, device_id_type=MESH,
         ).start()
 
+    for_peers(group, send_rows)
+
+    for load in loads[2:]:
+        load.wait()
     nblk = dets * per_det
     hits = hit_ref[...]
-    live = count_ref[...]
+    live = jnp.sum(
+        jnp.where(
+            lax.broadcasted_iota(jnp.int32, (owners, owners), 0)
+            == lax.broadcasted_iota(jnp.int32, (owners, owners), 1),
+            jnp.broadcast_to(count_ref[...].astype(jnp.float32), (owners, owners)),
+            0.0,
+        ),
+        axis=1, keepdims=True,
+    ).astype(jnp.int32)
     blk = lax.broadcasted_iota(jnp.int32, (owners, nblk), 1)
     owner_id = lax.broadcasted_iota(jnp.int32, (owners, nblk), 0) + 1
     named = jnp.zeros((owners, nblk), jnp.int32)
@@ -184,14 +240,15 @@
         return (acc[:rows_up] + acc[rows_up:]).reshape(owners, up_count, LANES)
 
     def send_tiles(out, landing, send_sem, recv_sem):
-        @pl.loop(1, total)
-        def _(step):
+        def send(step):
             o, dev = any_peer(step)
             pltpu.make_async_remote_copy(
                 src_ref=out.at[o], dst_ref=landing.at[step - 1],
                 send_sem=send_sem, recv_sem=recv_sem, device_id=dev, device_id_type=MESH,
             ).start()
 
+        for_peers(total, send)
+
     def wait_all(ref, sem):
         pltpu.make_async_copy(ref, ref, sem).wait()
 
@@ -201,13 +258,14 @@
         mine = mine + red_in[step]
     full[me_group] = mine
 
-    @pl.loop(1, group)
-    def _(step):
+    def send_sums(step):
         g, dev = group_peer(step)
         pltpu.make_async_remote_copy(
             src_ref=full.at[me_group], dst_ref=full.at[me_group],
             send_sem=all_send, recv_sem=all_recv, device_id=dev, device_id_type=MESH,
         ).start()
+
+    for_peers(group, send_sums)
 
     split(weight)
     wgt_out[...] = bin_all()
@@ -243,7 +301,7 @@
     total = group * n_waf
     dets, samp = tod.shape[1:]
     templ = templates.shape[1]
-    owners = hitlist.shape[1]
+    owners, slots = hitlist.shape[1:]
     part = templ // group
     up_count = TILE // LANES
     vmem = pl.BlockSpec(memory_space=pltpu.VMEM)
@@ -252,9 +310,15 @@
     out = pl.pallas_call(
         functools.partial(kernel, sizes),
         out_shape=jax.ShapeDtypeStruct((up_count, LANES), f32),
-        in_specs=[vmem] * 6,
+        in_specs=[pl.BlockSpec(memory_space=pltpu.HBM)] * 6,
         out_specs=vmem,
         scratch_shapes=[
+            pltpu.VMEM((dets, samp), f32),
+            pltpu.VMEM((templ, samp), f32),
+            pltpu.VMEM((1, dets), f32),
+            pltpu.VMEM((dets, samp), i32),
+            pltpu.VMEM((owners, slots), i32),
+            pltpu.VMEM((1, owners), i32),
             pltpu.VMEM((group, part, wide), f32),
             pltpu.VMEM((group - 1, part, wide), f32),
             pltpu.VMEM((group, part, wide), f32),
@@ -267,11 +331,12 @@
             pltpu.VMEM((total - 1, up_count, LANES), f32),
             pltpu.VMEM((total - 1, up_count, LANES), f32),
         ]
-        + [pltpu.SemaphoreType.DMA] * 8,
+        + [pltpu.SemaphoreType.DMA] * 8
+        + [pltpu.SemaphoreType.DMA((6,))],
         compiler_params=pltpu.CompilerParams(
-            collective_id=0, has_side_effects=True, vmem_limit_bytes=32 * 1024 * 1024
+            collective_id=0, has_side_effects=True, vmem_limit_bytes=63 * 1024 * 1024
         ),
-    )(tod[0], templates[0], det_weight[None, :], pixel[0], hitlist[0], counts[0])
+    )(tod[0], templates[0], det_weight[None, :], pixel[0], hitlist[0], counts[0].T)
     return out.reshape(-1)
 
 

time: 28.3 us -> 25.4 us (0.90)
  local copies, waits for them, and re-layouts: 4.41 us -> 1.26 us
  Pallas kernels: 23.6 us -> 24 us
    unnamed x13 -> x1, local copies, waits for them, and re-layouts: 4.32 us -> 1.26 us
    pallas_call x1, Pallas kernels: 23.6 us -> 24 us  [shards(): pl.pallas_call(functools.partial(kernel, sizes), out_shape=jax.ShapeDtype...]
where the time goes in v2:
time: 25.4 us; the launch traced here: 25.3 us
  Pallas kernels  24 us (94%)
  local copies, waits for them, and re-layouts  1.26 us (5%)
    pallas_call x1, Pallas kernels, shards(): pl.pallas_call(functools.partial(kernel, sizes), out_shape=jax.ShapeDtype...  24 us
    unnamed x1, local copies, waits for them, and re-layouts  1.26 us

profile of v2, /device:TPU:0, one launch (start us, length us, event | category | flops | bytes accessed | tf_op | source)
XLA Modules:
  0.0 25.3 jit_solution(3312890774241479467)
XLA Ops:
  0.0 24.0 %shard_map.64 = f32[4,128]{1,0:T(4,128)} custom-call(f32[64,256]{1,0:T(8,128)} %bitcast.7, f32[64,256]{1,0:T(8,128)} %bitcast.8, f32[1,64]{1,0:T(1,128)} %bitcast.12, s32[64,256]{1,0:T(8,128)} %bitcast.9, s32[16,16]{1,0:T(8,128)} %bitcast.11, s32[1,16]{1,0:T(1,128)} %bitcast.13), custom_call_target="tpu_custom_call" | custom-call | tf_op jit(solution)/shard_map/pallas_call | solution.py:310
  24.0 1.3 %copy.8 = f32[512]{0:T(512)} copy(f32[512]{0:T(512)} %bitcast.10) | data formatting | bytes 4096

commit v3 on v2

--- a/solution.py
+++ b/solution.py
@@ -77,6 +77,8 @@
     num_send,
     num_recv,
     load_sems,
+    low_hot,
+    up_hot,
 ):
     n_sec, n_waf, n_sub = sizes
     group = n_sec * n_sub
@@ -214,26 +216,42 @@
         vals_hi[...] = hi
         vals_lo[...] = values - hi
 
+    span = 8 * samp
+    up_iota = lax.broadcasted_iota(jnp.int32, (rows_up, samp), 0)
+    low_iota = lax.broadcasted_iota(jnp.int32, (LANES, samp), 0)
+
+    def build(c, carry):
+        d0 = pl.multiple_of(c * 8, 8)
+        u8 = upper[pl.ds(d0, 8), :]
+        l8 = lower[pl.ds(d0, 8), :]
+        ups, lows = [], []
+        for i in range(8):
+            ups.append((u8[i : i + 1, :] == up_iota).astype(jnp.float32).astype(jnp.bfloat16))
+            hot = (l8[i : i + 1, :] == low_iota).astype(jnp.float32)
+            lows.append(jnp.transpose(hot).astype(jnp.bfloat16))
+        k0 = pl.multiple_of(c * span, span)
+        low_hot[pl.ds(k0, span), :] = jnp.concatenate(lows, axis=0)
+        r0 = pl.multiple_of(c * rows_up, rows_up)
+        up_hot[pl.ds(r0, rows_up), :] = jnp.concatenate(ups, axis=1)
+        return carry
+
     def bin_all():
-        up_iota = lax.broadcasted_iota(jnp.int32, (rows_up, samp), 0)
-        low_iota = lax.broadcasted_iota(jnp.int32, (LANES, samp), 0)
+        def spread(row):
+            tile16 = jnp.broadcast_to(row, (16, samp)).astype(jnp.bfloat16)
+            return jnp.concatenate([tile16] * (rows_up // 16), axis=0)
 
         def body(c, acc):
             d0 = pl.multiple_of(c * 8, 8)
-            u8 = upper[pl.ds(d0, 8), :]
-            l8 = lower[pl.ds(d0, 8), :]
             h8 = vals_hi[pl.ds(d0, 8), :]
             o8 = vals_lo[pl.ds(d0, 8), :]
-            lhs, rhs = [], []
-            for i in range(8):
-                hot = u8[i : i + 1, :] == up_iota
-                a_hi = jnp.where(hot, h8[i : i + 1, :], 0.0).astype(jnp.bfloat16)
-                a_lo = jnp.where(hot, o8[i : i + 1, :], 0.0).astype(jnp.bfloat16)
-                lhs.append(jnp.concatenate([a_hi, a_lo], axis=0))
-                rhs.append((l8[i : i + 1, :] == low_iota).astype(jnp.float32).astype(jnp.bfloat16))
+            r0 = pl.multiple_of(c * rows_up, rows_up)
+            hot = up_hot[pl.ds(r0, rows_up), :]
+            his = jnp.concatenate([spread(h8[i : i + 1, :]) for i in range(8)], axis=1)
+            los = jnp.concatenate([spread(o8[i : i + 1, :]) for i in range(8)], axis=1)
+            k0 = pl.multiple_of(c * span, span)
             return acc + lax.dot_general(
-                jnp.concatenate(lhs, axis=1), jnp.concatenate(rhs, axis=1),
-                (((1,), (1,)), ((), ())), preferred_element_type=jnp.float32,
+                jnp.concatenate([hot * his, hot * los], axis=0), low_hot[pl.ds(k0, span), :],
+                (((1,), (0,)), ((), ())), preferred_element_type=jnp.float32,
             )
 
         acc = lax.fori_loop(0, dets // 8, body, jnp.zeros((2 * rows_up, LANES), jnp.float32))
@@ -252,6 +270,7 @@
     def wait_all(ref, sem):
         pltpu.make_async_copy(ref, ref, sem).wait()
 
+    lax.fori_loop(0, dets // 8, build, 0)
     wait_all(red_in, red_recv)
     mine = aug[me_group]
     for step in range(group - 1):
@@ -332,7 +351,11 @@
             pltpu.VMEM((total - 1, up_count, LANES), f32),
         ]
         + [pltpu.SemaphoreType.DMA] * 8
-        + [pltpu.SemaphoreType.DMA((6,))],
+        + [
+            pltpu.SemaphoreType.DMA((6,)),
+            pltpu.VMEM((dets * samp, LANES), jnp.bfloat16),
+            pltpu.VMEM((dets // 8 * owners * up_count, 8 * samp), jnp.bfloat16),
+        ],
         compiler_params=pltpu.CompilerParams(
             collective_id=0, has_side_effects=True, vmem_limit_bytes=63 * 1024 * 1024
         ),

time: 25.4 us -> 25.1 us (0.988)
  Pallas kernels: 24 us -> 23.7 us
    pallas_call x1, Pallas kernels: 24 us -> 23.7 us  [shards(): pl.pallas_call(functools.partial(kernel, sizes), out_shape=jax.ShapeDtype...]
where the time goes in v3:
time: 25.1 us; the launch traced here: 25 us
  Pallas kernels  23.7 us (94%)
  local copies, waits for them, and re-layouts  1.26 us (5%)
    pallas_call x1, Pallas kernels, shards(): pl.pallas_call(functools.partial(kernel, sizes), out_shape=jax.ShapeDtype...  23.7 us
    unnamed x1, local copies, waits for them, and re-layouts  1.26 us

profile of v3, /device:TPU:0, one launch (start us, length us, event | category | flops | bytes accessed | tf_op | source)
XLA Modules:
  0.0 25.0 jit_solution(8209283991798237539)
XLA Ops:
  0.0 23.7 %shard_map.64 = f32[4,128]{1,0:T(4,128)} custom-call(f32[64,256]{1,0:T(8,128)} %bitcast.7, f32[64,256]{1,0:T(8,128)} %bitcast.8, f32[1,64]{1,0:T(1,128)} %bitcast.12, s32[64,256]{1,0:T(8,128)} %bitcast.9, s32[16,16]{1,0:T(8,128)} %bitcast.11, s32[1,16]{1,0:T(1,128)} %bitcast.13), custom_call_target="tpu_custom_call" | custom-call | tf_op jit(solution)/shard_map/pallas_call | solution.py:329
  23.7 1.3 %copy.8 = f32[512]{0:T(512)} copy(f32[512]{0:T(512)} %bitcast.10) | data formatting | bytes 4096
